TPU v7x, 128 devices: a whole 4x4x4 slice. The times are simulated.
128 devices in a mesh: sa: 8 (over z, y_hi), sb: 16 (over x, y_lo, core).
Axes of the slice: x: 4, y: 4 (y_hi: 2, y_lo: 2; y = y_hi * 2 + y_lo), z: 4, core: 2. Of those that a mesh axis runs over, the one named last changes fastest.
Arguments:
- queries: float32 [32768, 128], P(('sa', 'sb')), may hold values from -6 to 6
- keys: float32 [32768, 128], P(('sa', 'sb')), may hold values from -6 to 6
- values: float32 [32768, 128], P(('sa', 'sb')), may hold values from -6 to 6
- cotangent: float32 [32768, 128], P(('sa', 'sb')), may hold values from -6 to 6
- filt: float32 [32768, 128], P(('sa', 'sb')), may hold values from -6 to 6
- skip: float32 [128], replicated, may hold values from -4 to 4
Outputs:
- grad_queries: float32 [32768, 128], P(('sa', 'sb'))
- grad_keys: float32 [32768, 128], P(('sa', 'sb'))
- grad_values: float32 [32768, 128], P(('sa', 'sb'))
- grad_filter: float32 [32768, 128], P(('sa', 'sb'))
All inputs are finite; a program needn't handle non-finite values.
Results may differ from a plain program's by a relative error of at most 0.000098.
Values sent between devices are 32-bit elements; how exact they have to be, the bound alone decides.
A program may use at most 64 MiB of HBM per device.

v0:
```python
import math

import jax
import jax.numpy as jnp
import numpy as np
from jax import lax
from jax.experimental import pallas as pl
from jax.experimental.pallas import tpu as pltpu
from jax.sharding import PartitionSpec as P

DEVICES = 128
BLOCK = 256
LENGTH = DEVICES * BLOCK
HALF = 128
ROWS = 6
LOGICAL = pl.DeviceIdType.LOGICAL
bfloat16 = jnp.bfloat16


def tables():
    s = np.arange(DEVICES, dtype=np.float64)
    r = np.arange(BLOCK, dtype=np.float64)
    outer = np.exp(-2j * np.pi * np.outer(s + 0.25, s) / DEVICES)
    turn = np.exp(-2j * np.pi * np.outer(s + 0.25, r) / LENGTH)
    inner = np.exp(-2j * np.pi * (np.outer(r, r) % BLOCK) / BLOCK)
    scale = 1.0 / (LENGTH * math.sqrt(LENGTH))
    spread = np.concatenate([outer.real, outer.imag], 0)
    gather = np.concatenate([outer.real.T, outer.imag.T], 1) * scale
    inners = np.concatenate([inner.real, inner.imag], 1)
    turns = np.concatenate([turn.real, turn.imag], 0)
    return tuple(table.astype(np.float32) for table in (spread, gather, inners, turns))


def hops(offset):
    ring = (0, 1, 2, 1)
    return ring[(offset >> 1) & 3] + ring[(offset >> 3) & 3] + ring[(offset >> 5) & 3]


ORDER = sorted(range(1, DEVICES), key=lambda offset: -hops(offset))


def split(x):
    high = x.astype(bfloat16)
    low = (x - high.astype(jnp.float32)).astype(bfloat16)
    return high, low


def dot(a, b):
    return jnp.dot(a, b, preferred_element_type=jnp.float32)


def exchange_kernel(
    q_hbm, k_hbm, v_hbm, c_hbm, f_hbm, spread_hbm, gather_hbm, inners_hbm, turns_hbm,
    forward_out, back_out, filter_out,
    ins, spread_table, gather_table, inners, turns, spread, gather, fh, fl, gh, gl, outgoing, arrived, results, returned,
    in_sem, const_sem, send_sem, recv_sem, own_sem,
):
    sa, sb = lax.axis_index("sa"), lax.axis_index("sb")
    me = sa * 16 + sb
    z, y = sa >> 1, ((sa & 1) << 1) | ((sb >> 1) & 1)
    x, core = sb >> 2, sb & 1
    z_part = [((z + d) & 3) << 5 for d in range(4)]
    y_part = [(((y + d) & 2) << 3) | (((y + d) & 1) << 1) for d in range(4)]
    x_part = [((x + d) & 3) << 2 for d in range(4)]
    core_part = [core, 1 - core]

    def peer(offset):
        return z_part[(offset >> 5) & 3] | y_part[(offset >> 3) & 3] | x_part[(offset >> 1) & 3] | core_part[offset & 1]

    barrier = pltpu.get_barrier_semaphore()
    for offset in ORDER:
        pl.semaphore_signal(barrier, 1, device_id=peer(offset), device_id_type=LOGICAL)
    loads = [
        pltpu.make_async_copy(ref, ins.at[i], in_sem.at[i]) for i, ref in enumerate((q_hbm, k_hbm, v_hbm, c_hbm, f_hbm))
    ]
    for load in loads:
        load.start()
    pairs = ((spread_hbm, spread_table), (gather_hbm, gather_table), (inners_hbm, inners), (turns_hbm, turns))
    constants = [pltpu.make_async_copy(a, b, const_sem.at[i]) for i, (a, b) in enumerate(pairs)]
    for load in constants:
        load.start()
    for load in loads:
        load.wait()
    signals = (ins[1] * ins[2], ins[4], ins[3] * ins[0])
    for number, signal in enumerate(signals):
        for half in range(2):
            outgoing[:, 2 * number + half, :] = signal[half * HALF : (half + 1) * HALF, :].T
    for load in constants:
        load.wait()
    for table, target in ((spread_table, spread), (gather_table, gather)):
        high, low = split(table[...])
        width = table.shape[1]
        target[:, :width] = high
        target[:, width : 2 * width] = high
        target[:, 2 * width :] = low
    real_high, real_low = split(inners[:, :BLOCK])
    imag_high, imag_low = split(inners[:, BLOCK:])
    for real, imag, forward, inverse in ((real_high, imag_high, fh, gh), (real_low, imag_low, fl, gl)):
        for table, right, left in ((forward, imag, -imag), (inverse, -imag, imag)):
            table[:BLOCK, :BLOCK] = real
            table[:BLOCK, BLOCK:] = right
            table[BLOCK:, :BLOCK] = left
            table[BLOCK:, BLOCK:] = real
    pl.semaphore_wait(barrier, DEVICES - 1)

    def exchange(source, target, phase):
        for offset in ORDER:
            other = peer(offset)
            pltpu.make_async_remote_copy(
                src_ref=source.at[other, pl.ds(0, ROWS)],
                dst_ref=target.at[me, pl.ds(0, ROWS)],
                send_sem=send_sem.at[phase],
                recv_sem=recv_sem.at[phase],
                device_id=other,
                device_id_type=LOGICAL,
            ).start()
        own = pltpu.make_async_copy(
            source.at[me, pl.ds(0, ROWS)], target.at[me, pl.ds(0, ROWS)], own_sem.at[phase]
        )
        own.start()
        own.wait()
        landed = target.at[pl.ds(0, DEVICES - 1), pl.ds(0, ROWS)]
        pltpu.make_async_copy(landed, landed, recv_sem.at[phase]).wait()

    exchange(outgoing, arrived, 0)

    signal = jnp.concatenate([arrived[:, row, :] for row in range(ROWS)], 1)
    high, low = split(signal)
    first = dot(spread[...], jnp.concatenate([high, low, high], 0))
    turn_real, turn_imag = turns[:HALF, :], turns[HALF:, :]
    turned = []
    for number in range(3):
        real = first[:HALF, number * BLOCK : (number + 1) * BLOCK]
        imag = first[HALF:, number * BLOCK : (number + 1) * BLOCK]
        turned.append(
            jnp.concatenate([real * turn_real - imag * turn_imag, real * turn_imag + imag * turn_real], 1)
        )
    high, low = split(jnp.concatenate(turned, 0))
    spectra = dot(high, fh[...]) + dot(low, fh[...]) + dot(high, fl[...])
    gr, gi = spectra[:HALF, :BLOCK], spectra[:HALF, BLOCK:]
    fr, fi = spectra[HALF : 2 * HALF, :BLOCK], spectra[HALF : 2 * HALF, BLOCK:]
    ur, ui = spectra[2 * HALF :, :BLOCK], spectra[2 * HALF :, BLOCK:]
    products = (
        jnp.concatenate([fr * gr - fi * gi, fr * gi + fi * gr], 1),
        jnp.concatenate([fr * ur + fi * ui, fr * ui - fi * ur], 1),
        jnp.concatenate([gr * ur + gi * ui, gr * ui - gi * ur], 1),
    )
    high, low = split(jnp.concatenate(products, 0))
    second = dot(high, gh[...]) + dot(low, gh[...]) + dot(high, gl[...])
    turned = []
    for number in range(3):
        real = second[number * HALF : (number + 1) * HALF, :BLOCK]
        imag = second[number * HALF : (number + 1) * HALF, BLOCK:]
        turned.append(
            jnp.concatenate([real * turn_real + imag * turn_imag, imag * turn_real - real * turn_imag], 0)
        )
    high, low = split(jnp.concatenate(turned, 1))
    convolved = dot(gather[...], jnp.concatenate([high, low, high], 0))
    for row in range(ROWS):
        results[:, row, :] = convolved[:, row * HALF : (row + 1) * HALF]

    exchange(results, returned, 1)
    for number, out in enumerate((forward_out, back_out, filter_out)):
        for half in range(2):
            out[half * HALF : (half + 1) * HALF, :] = returned[:, 2 * number + half, :].T
    for phase, source in enumerate((outgoing, results)):
        sent = source.at[pl.ds(0, DEVICES - 1), pl.ds(0, ROWS)]
        pltpu.make_async_copy(sent, sent, send_sem.at[phase]).wait()


def local(queries, keys, values, cotangent, filt, skip):
    constants = tables()
    block = jax.ShapeDtypeStruct((BLOCK, DEVICES), jnp.float32)
    buffer = pltpu.VMEM((DEVICES, 8, HALF), jnp.float32)
    forward_conv, back_conv, filter_conv = pl.pallas_call(
        exchange_kernel,
        out_shape=(block, block, block),
        in_specs=[pl.BlockSpec(memory_space=pl.ANY)] * 9,
        out_specs=[pl.BlockSpec(memory_space=pltpu.VMEM)] * 3,
        scratch_shapes=[
            pltpu.VMEM((5, BLOCK, DEVICES), jnp.float32),
            *[pltpu.VMEM(c.shape, jnp.float32) for c in constants],
            pltpu.VMEM((BLOCK, 3 * DEVICES), bfloat16),
            pltpu.VMEM((DEVICES, 3 * BLOCK), bfloat16),
            *[pltpu.VMEM((2 * BLOCK, 2 * BLOCK), bfloat16)] * 4,
            buffer, buffer, buffer, buffer,
            pltpu.SemaphoreType.DMA((5,)),
            pltpu.SemaphoreType.DMA((4,)),
            pltpu.SemaphoreType.DMA((2,)),
            pltpu.SemaphoreType.DMA((2,)),
            pltpu.SemaphoreType.DMA((2,)),
        ],
        compiler_params=pltpu.CompilerParams(
            collective_id=0, has_side_effects=True, vmem_limit_bytes=60 * 1024 * 1024
        ),
        name="channel_convolutions",
    )(queries, keys, values, cotangent, filt, *[jnp.asarray(c) for c in constants])
    response = forward_conv + skip * (keys * values)
    back_signal = back_conv + skip * (cotangent * queries)
    return (cotangent * response, back_signal * values, back_signal * keys, filter_conv)


def solution(mesh):
    in_specs = (P(("sa", "sb"), None),) * 5 + (P(),)
    out_specs = (P(("sa", "sb"), None),) * 4
    return jax.shard_map(local, mesh=mesh, in_specs=in_specs, out_specs=out_specs, check_vma=False)
```

profile of v0, /device:TPU:1, one launch (start us, length us, event | category | flops | bytes accessed | tf_op | source)
XLA Modules:
  0.0 33.9 jit_solution(6335040271864087473)
XLA Ops:
  0.6 0.0 copy-start
  0.6 0.0 copy-start.3
  0.7 0.0 copy-start.1
  0.7 0.0 copy-start.2
  0.7 29.2 %channel_convolutions.1 = (f32[256,128]{1,0:T(8,128)}, f32[256,128]{1,0:T(8,128)}, f32[256,128]{1,0:T(8,128)}) custom-call(f32[256,128]{1,0:T(8,128)} %q_hbm.1, f32[256,128]{1,0:T(8,128)} %k_hbm.1, f32[256,128]{1,0:T(8,128)} %v_hbm.1, f32[256,128]{1,0:T(8,128)} %c_hbm.1, f32[256,128]{1,0:T(8,128)} %f_hbm.1, f32[256,128]{1,0:T(8,128)} %constant.8.clone.spread_hbm, ...), custom_call_target="tpu_custom_call" | custom-call | tf_op jit(solution)/shard_map/channel_convolutions/pallas_call | solution.py:175
  29.9 0.0 copy-start.5
  29.9 0.0 copy-done
  29.9 0.0 copy-done.3
  29.9 0.0 copy-done.1
  29.9 0.0 copy-done.2
  29.9 0.6 %copy-done.5 = f32[128]{0:T(128)S(1)} copy-done((f32[128]{0:T(128)S(1)}, f32[128]{0:T(128)}, u32[]{:S(2)}) %copy-start.5) | copy-done | bytes 536
  30.5 1.7 %fusion = (f32[256,128]{1,0:T(8,128)}, f32[256,128]{1,0:T(8,128)S(1)}, f32[256,128]{1,0:T(8,128)}) fusion(f32[256,128]{1,0:T(8,128)S(1)} %copy-done.1, f32[256,128]{1,0:T(8,128)} %get-tuple-element.8, f32[256,128]{1,0:T(8,128)S(1)} %copy-done.3, f32[256,128]{1,0:T(8,128)S(1)} %copy-done.2, f32[128]{0:T(128)S(1)} %copy-done.5, ...), kind=kLoop, calls=%fused_computation.2 | loop fusion | flops 262144 | bytes 1180160 | tf_op jit(solution)/shard_map/mul | solution.py:200
  32.3 0.0 copy-start.4
  32.3 0.7 %mul.35 = f32[256,128]{1,0:T(8,128)} multiply(f32[256,128]{1,0:T(8,128)S(1)} %get-tuple-element.11, f32[256,128]{1,0:T(8,128)S(1)} %copy-done) | non-fusion elementwise | flops 32768 | bytes 393216 | tf_op jit(solution)/shard_map/mul | solution.py:200
  32.9 0.3 copy-done.4
  33.2 0.7 %copy.15 = f32[256,128]{1,0:T(8,128)} copy(f32[256,128]{1,0:T(8,128)S(1)} %copy-done.4) | data formatting | bytes 262144
Async XLA Ops:
  0.6 29.3 %copy-start = (f32[256,128]{1,0:T(8,128)S(1)}, f32[256,128]{1,0:T(8,128)}, u32[]{:S(2)}) copy-start(f32[256,128]{1,0:T(8,128)} %v_hbm.1) | copy-start | bytes 393220
  0.6 29.3 %copy-start.3 = (f32[256,128]{1,0:T(8,128)S(1)}, f32[256,128]{1,0:T(8,128)}, u32[]{:S(2)}) copy-start(f32[256,128]{1,0:T(8,128)} %c_hbm.1) | copy-start | bytes 393220
  0.7 29.3 %copy-start.1 = (f32[256,128]{1,0:T(8,128)S(1)}, f32[256,128]{1,0:T(8,128)}, u32[]{:S(2)}) copy-start(f32[256,128]{1,0:T(8,128)} %k_hbm.1) | copy-start | bytes 393220
  0.7 29.3 %copy-start.2 = (f32[256,128]{1,0:T(8,128)S(1)}, f32[256,128]{1,0:T(8,128)}, u32[]{:S(2)}) copy-start(f32[256,128]{1,0:T(8,128)} %q_hbm.1) | copy-start | bytes 393220
  29.9 0.7 %copy-start.5 = (f32[128]{0:T(128)S(1)}, f32[128]{0:T(128)}, u32[]{:S(2)}) copy-start(f32[128]{0:T(128)} %param.15) | copy-start | bytes 1540
  32.3 1.0 %copy-start.4 = (f32[256,128]{1,0:T(8,128)S(1)}, f32[256,128]{1,0:T(8,128)}, u32[]{:S(2)}) copy-start(f32[256,128]{1,0:T(8,128)} %get-tuple-element.20) | copy-start | bytes 393220
where the time goes:
time: 34 us; the launch traced here: 33.9 us
  Pallas kernels  29.2 us (86%)
  other arithmetic  2.38 us (7%)
  local copies, waits for them, and re-layouts  1.56 us (5%)
  between operations  0.71 us (2%)
    pallas_call x1, Pallas kernels, local(): pl.pallas_call(exchange_kernel, out_shape=(block, block, block), in_specs...  29.2 us
    mul x1, other arithmetic, local(): back_signal * keys  1.71 us
    unnamed x13, local copies, waits for them, and re-layouts  1.56 us

commit v1 on v0

--- a/solution.py
+++ b/solution.py
@@ -37,6 +37,9 @@
 
 
 ORDER = sorted(range(1, DEVICES), key=lambda offset: -hops(offset))
+NEAR = [offset for offset in ORDER if hops(offset) <= 3]
+FAR = [offset for offset in ORDER if hops(offset) > 3]
+RELAYS = (0b0101010, 0b1111110)
 
 
 def split(x):
@@ -50,10 +53,10 @@
 
 
 def exchange_kernel(
-    q_hbm, k_hbm, v_hbm, c_hbm, f_hbm, spread_hbm, gather_hbm, inners_hbm, turns_hbm,
-    forward_out, back_out, filter_out,
-    ins, spread_table, gather_table, inners, turns, spread, gather, fh, fl, gh, gl, outgoing, arrived, results, returned,
-    in_sem, const_sem, send_sem, recv_sem, own_sem,
+    q_hbm, k_hbm, v_hbm, c_hbm, f_hbm, skip_hbm, spread_hbm, gather_hbm, inners_hbm, turns_hbm,
+    returned, ins,
+    skip, spread_table, gather_table, inners, turns, spread, gather, fh, fl, gh, gl, outgoing, arrived, results,
+    in_sem, const_sem, send_sem, recv_sem, own_sem, relay_sem,
 ):
     sa, sb = lax.axis_index("sa"), lax.axis_index("sb")
     me = sa * 16 + sb
@@ -67,24 +70,56 @@
     def peer(offset):
         return z_part[(offset >> 5) & 3] | y_part[(offset >> 3) & 3] | x_part[(offset >> 1) & 3] | core_part[offset & 1]
 
-    barrier = pltpu.get_barrier_semaphore()
-    for offset in ORDER:
-        pl.semaphore_signal(barrier, 1, device_id=peer(offset), device_id_type=LOGICAL)
     loads = [
         pltpu.make_async_copy(ref, ins.at[i], in_sem.at[i]) for i, ref in enumerate((q_hbm, k_hbm, v_hbm, c_hbm, f_hbm))
     ]
+    loads.append(pltpu.make_async_copy(skip_hbm, skip, in_sem.at[5]))
     for load in loads:
         load.start()
+    barrier = pltpu.get_barrier_semaphore()
+    for offset in NEAR:
+        pl.semaphore_signal(barrier, 1, device_id=peer(offset), device_id_type=LOGICAL)
     pairs = ((spread_hbm, spread_table), (gather_hbm, gather_table), (inners_hbm, inners), (turns_hbm, turns))
     constants = [pltpu.make_async_copy(a, b, const_sem.at[i]) for i, (a, b) in enumerate(pairs)]
     for load in constants:
         load.start()
     for load in loads:
         load.wait()
-    signals = (ins[1] * ins[2], ins[4], ins[3] * ins[0])
-    for number, signal in enumerate(signals):
+    gated, upstream = ins[1] * ins[2], ins[3] * ins[0]
+    for number, signal in enumerate((gated, ins[4], upstream)):
         for half in range(2):
             outgoing[:, 2 * number + half, :] = signal[half * HALF : (half + 1) * HALF, :].T
+    pl.semaphore_wait(barrier, len(NEAR))
+    for offset in RELAYS:
+        pl.semaphore_signal(relay_sem, 1, device_id=peer(offset), device_id_type=LOGICAL)
+
+    def send(source, target, phase, offsets):
+        for offset in offsets:
+            other = peer(offset)
+            pltpu.make_async_remote_copy(
+                src_ref=source.at[other, pl.ds(0, ROWS)],
+                dst_ref=target.at[me, pl.ds(0, ROWS)],
+                send_sem=send_sem.at[phase],
+                recv_sem=recv_sem.at[phase],
+                device_id=other,
+                device_id_type=LOGICAL,
+            ).start()
+
+    def receive(source, target, phase):
+        own = pltpu.make_async_copy(
+            source.at[me, pl.ds(0, ROWS)], target.at[me, pl.ds(0, ROWS)], own_sem.at[phase]
+        )
+        own.start()
+        own.wait()
+        landed = target.at[pl.ds(0, DEVICES - 1), pl.ds(0, ROWS)]
+        pltpu.make_async_copy(landed, landed, recv_sem.at[phase]).wait()
+
+    send(outgoing, arrived, 0, NEAR)
+    pl.semaphore_wait(relay_sem, len(RELAYS))
+    send(outgoing, arrived, 0, FAR)
+
+    ins[0] = skip[...][None, :] * upstream
+    ins[4] = skip[...][None, :] * gated
     for load in constants:
         load.wait()
     for table, target in ((spread_table, spread), (gather_table, gather)):
@@ -101,28 +136,7 @@
             table[:BLOCK, BLOCK:] = right
             table[BLOCK:, :BLOCK] = left
             table[BLOCK:, BLOCK:] = real
-    pl.semaphore_wait(barrier, DEVICES - 1)
-
-    def exchange(source, target, phase):
-        for offset in ORDER:
-            other = peer(offset)
-            pltpu.make_async_remote_copy(
-                src_ref=source.at[other, pl.ds(0, ROWS)],
-                dst_ref=target.at[me, pl.ds(0, ROWS)],
-                send_sem=send_sem.at[phase],
-                recv_sem=recv_sem.at[phase],
-                device_id=other,
-                device_id_type=LOGICAL,
-            ).start()
-        own = pltpu.make_async_copy(
-            source.at[me, pl.ds(0, ROWS)], target.at[me, pl.ds(0, ROWS)], own_sem.at[phase]
-        )
-        own.start()
-        own.wait()
-        landed = target.at[pl.ds(0, DEVICES - 1), pl.ds(0, ROWS)]
-        pltpu.make_async_copy(landed, landed, recv_sem.at[phase]).wait()
-
-    exchange(outgoing, arrived, 0)
+    receive(outgoing, arrived, 0)
 
     signal = jnp.concatenate([arrived[:, row, :] for row in range(ROWS)], 1)
     high, low = split(signal)
@@ -159,45 +173,71 @@
     for row in range(ROWS):
         results[:, row, :] = convolved[:, row * HALF : (row + 1) * HALF]
 
-    exchange(results, returned, 1)
-    for number, out in enumerate((forward_out, back_out, filter_out)):
-        for half in range(2):
-            out[half * HALF : (half + 1) * HALF, :] = returned[:, 2 * number + half, :].T
+    send(results, returned, 1, ORDER)
+    receive(results, returned, 1)
     for phase, source in enumerate((outgoing, results)):
         sent = source.at[pl.ds(0, DEVICES - 1), pl.ds(0, ROWS)]
         pltpu.make_async_copy(sent, sent, send_sem.at[phase]).wait()
 
 
+def finish_kernel(returned, ins, gq_hbm, gk_hbm, gv_hbm, gf_hbm, outs, sems):
+    copies = []
+    for half in range(2):
+        rows = pl.ds(half * HALF, HALF)
+        response = returned[:, half, :].T + ins[4, rows, :]
+        back_signal = returned[:, 2 + half, :].T + ins[0, rows, :]
+        outs[0, rows, :] = ins[3, rows, :] * response
+        outs[1, rows, :] = back_signal * ins[2, rows, :]
+        outs[2, rows, :] = back_signal * ins[1, rows, :]
+        outs[3, rows, :] = returned[:, 4 + half, :].T
+        for i, out in enumerate((gq_hbm, gk_hbm, gv_hbm, gf_hbm)):
+            copies.append(pltpu.make_async_copy(outs.at[i, rows], out.at[rows], sems.at[i, half]))
+            copies[-1].start()
+    for copy in copies:
+        copy.wait()
+
+
 def local(queries, keys, values, cotangent, filt, skip):
     constants = tables()
+    buffer = jax.ShapeDtypeStruct((DEVICES, 8, HALF), jnp.float32)
     block = jax.ShapeDtypeStruct((BLOCK, DEVICES), jnp.float32)
-    buffer = pltpu.VMEM((DEVICES, 8, HALF), jnp.float32)
-    forward_conv, back_conv, filter_conv = pl.pallas_call(
+    five = jax.ShapeDtypeStruct((5, BLOCK, DEVICES), jnp.float32)
+    returned, kept = pl.pallas_call(
         exchange_kernel,
-        out_shape=(block, block, block),
-        in_specs=[pl.BlockSpec(memory_space=pl.ANY)] * 9,
-        out_specs=[pl.BlockSpec(memory_space=pltpu.VMEM)] * 3,
+        out_shape=(buffer, five),
+        in_specs=[pl.BlockSpec(memory_space=pltpu.HBM)] * 10,
+        out_specs=[pl.BlockSpec(memory_space=pltpu.VMEM)] * 2,
         scratch_shapes=[
-            pltpu.VMEM((5, BLOCK, DEVICES), jnp.float32),
+            pltpu.VMEM((DEVICES,), jnp.float32),
             *[pltpu.VMEM(c.shape, jnp.float32) for c in constants],
             pltpu.VMEM((BLOCK, 3 * DEVICES), bfloat16),
             pltpu.VMEM((DEVICES, 3 * BLOCK), bfloat16),
             *[pltpu.VMEM((2 * BLOCK, 2 * BLOCK), bfloat16)] * 4,
-            buffer, buffer, buffer, buffer,
-            pltpu.SemaphoreType.DMA((5,)),
+            *[pltpu.VMEM(buffer.shape, buffer.dtype)] * 3,
+            pltpu.SemaphoreType.DMA((6,)),
             pltpu.SemaphoreType.DMA((4,)),
             pltpu.SemaphoreType.DMA((2,)),
             pltpu.SemaphoreType.DMA((2,)),
             pltpu.SemaphoreType.DMA((2,)),
+            pltpu.SemaphoreType.REGULAR,
         ],
         compiler_params=pltpu.CompilerParams(
-            collective_id=0, has_side_effects=True, vmem_limit_bytes=60 * 1024 * 1024
+            collective_id=0, has_side_effects=True, vmem_limit_bytes=40 * 1024 * 1024
         ),
         name="channel_convolutions",
-    )(queries, keys, values, cotangent, filt, *[jnp.asarray(c) for c in constants])
-    response = forward_conv + skip * (keys * values)
-    back_signal = back_conv + skip * (cotangent * queries)
-    return (cotangent * response, back_signal * values, back_signal * keys, filter_conv)
+    )(*[
+        pltpu.with_memory_space_constraint(operand, pltpu.HBM)
+        for operand in (queries, keys, values, cotangent, filt, skip, *map(jnp.asarray, constants))
+    ])
+    return pl.pallas_call(
+        finish_kernel,
+        out_shape=(block,) * 4,
+        in_specs=[pl.BlockSpec(memory_space=pltpu.VMEM)] * 2,
+        out_specs=[pl.BlockSpec(memory_space=pltpu.HBM)] * 4,
+        scratch_shapes=[pltpu.VMEM((4, BLOCK, DEVICES), jnp.float32), pltpu.SemaphoreType.DMA((4, 2))],
+        compiler_params=pltpu.CompilerParams(vmem_limit_bytes=8 * 1024 * 1024),
+        name="gates",
+    )(returned, kept)
 
 
 def solution(mesh):

time: 34 us -> 31 us (0.912)
  other arithmetic: 2.38 us -> 0 us
  local copies, waits for them, and re-layouts: 1.56 us -> 0 us
  Pallas kernels: 29.2 us -> 30.2 us
    mul x2 -> x0, other arithmetic: 2.38 us -> none  [the longest x1 1.71 us: local(): back_signal * keys]
    unnamed x13 -> x0, local copies, waits for them, and re-layouts: 1.56 us -> none
    pallas_call x1 -> x2, Pallas kernels: 29.2 us -> 30.2 us  [the longest x1 29.1 us: local(): pl.pallas_call(exchange_kernel, out_shape=(buffer, five), in_specs=[pl.Bl...]
where the time goes in v1:
time: 31 us; the launch traced here: 30.8 us
  Pallas kernels  30.2 us (97%)
  between operations  0.64 us (2%)
    pallas_call x1, Pallas kernels, local(): pl.pallas_call(exchange_kernel, out_shape=(buffer, five), in_specs=[pl.Bl...  29.1 us
    pallas_call x1, Pallas kernels, local(): pl.pallas_call(finish_kernel, out_shape=(block,) * 4, in_specs=[pl.BlockS...  1.06 us

profile of v1, /device:TPU:1, one launch (start us, length us, event | category | flops | bytes accessed | tf_op | source)
XLA Modules:
  0.0 30.8 jit_solution(10895991007944513839)
XLA Ops:
  0.6 29.1 %channel_convolutions.1 = (f32[128,8,128]{2,1,0:T(8,128)S(1)}, f32[5,256,128]{2,1,0:T(8,128)S(1)}) custom-call(f32[256,128]{1,0:T(8,128)} %q_hbm.1, f32[256,128]{1,0:T(8,128)} %k_hbm.1, f32[256,128]{1,0:T(8,128)} %v_hbm.1, f32[256,128]{1,0:T(8,128)} %c_hbm.1, f32[256,128]{1,0:T(8,128)} %f_hbm.1, f32[128]{0:T(128)} %skip_hbm.1, ...), custom_call_target="tpu_custom_call" | custom-call | tf_op jit(solution)/shard_map/channel_convolutions/pallas_call | solution.py:205
  29.8 1.1 %gates.1 = (f32[256,128]{1,0:T(8,128)}, f32[256,128]{1,0:T(8,128)}, f32[256,128]{1,0:T(8,128)}, f32[256,128]{1,0:T(8,128)}) custom-call(f32[128,8,128]{2,1,0:T(8,128)S(1)} %get-tuple-element.6.returned, f32[5,256,128]{2,1,0:T(8,128)S(1)} %get-tuple-element.7.ins), custom_call_target="tpu_custom_call" | custom-call | tf_op jit(solution)/shard_map/gates/pallas_call | solution.py:232

commit v2 on v1

v2 whole, which is shorter than its diff:
```python
import math

import jax
import jax.numpy as jnp
import numpy as np
from jax import lax
from jax.experimental import pallas as pl
from jax.experimental.pallas import tpu as pltpu
from jax.sharding import PartitionSpec as P

DEVICES = 128
BLOCK = 256
LENGTH = DEVICES * BLOCK
HALF = 128
ROWS = 6
LOGICAL = pl.DeviceIdType.LOGICAL
bfloat16 = jnp.bfloat16
RING = (0, 1, 2, 1)
BEHIND = (0.0, 2.0, 2.5, 2.9), (0.0, 0.8, 1.1, 1.0)

def tables():
    s = np.arange(DEVICES, dtype=np.float64)
    r = np.arange(BLOCK, dtype=np.float64)
    half = r[:HALF]
    outer = np.exp(-2j * np.pi * np.outer(s + 0.25, s) / DEVICES)
    turn = np.exp(-2j * np.pi * np.outer(s + 0.25, r) / LENGTH)
    inner = np.exp(-2j * np.pi * (np.outer(half, half) % HALF) / HALF)
    twist = np.exp(-2j * np.pi * half / BLOCK)
    scale = 1.0 / (LENGTH * math.sqrt(LENGTH))
    spread = np.concatenate([outer.real, outer.imag], 0)
    gather = np.concatenate([outer.real.T, outer.imag.T], 1) * scale
    inners = np.concatenate([inner.real, inner.imag], 1)
    turns = np.concatenate([turn.real, turn.imag], 0)
    twists = np.zeros((8, HALF))
    twists[0], twists[1] = twist.real, twist.imag
    return tuple(table.astype(np.float32) for table in (spread, gather, inners, turns, twists))


def hops(offset):
    return RING[(offset >> 1) & 3] + RING[(offset >> 3) & 3] + RING[(offset >> 5) & 3]


def returns():
    places = [(z, y, x, c) for z in range(4) for y in range(4) for x in range(4) for c in (1, 0)]
    return sorted(places, key=lambda p: (BEHIND[0][p[0]] + BEHIND[1][p[2]] - 0.64 * RING[p[1]], -p[3]))


ORDER = sorted(range(1, DEVICES), key=lambda offset: (-hops(offset), (offset * 77) % DEVICES))


def split(x):
    high = x.astype(bfloat16)
    low = (x - high.astype(jnp.float32)).astype(bfloat16)
    return high, low


def dot(a, b):
    return jnp.dot(a, b, preferred_element_type=jnp.float32)


def product(a, b, conjugate):
    ar, ai, br, bi = a[:, :HALF], a[:, HALF:], b[:, :HALF], b[:, HALF:]
    if conjugate:
        return jnp.concatenate([ar * br + ai * bi, ar * bi - ai * br], 1)
    return jnp.concatenate([ar * br - ai * bi, ar * bi + ai * br], 1)


def exchange_kernel(
    q_hbm, k_hbm, v_hbm, c_hbm, f_hbm, skip_hbm, spread_hbm, gather_hbm, inners_hbm, turns_hbm, twists_hbm,
    returned, ins,
    skip, spread_table, gather_table, inners, turns, twists, spread, gather, forward, inverse,
    outgoing, arrived, results,
    in_sem, const_sem, send_sem, recv_sem, own_sem,
):
    sa, sb = lax.axis_index("sa"), lax.axis_index("sb")
    me = sa * 16 + sb
    z, y = sa >> 1, ((sa & 1) << 1) | ((sb >> 1) & 1)
    x, core = sb >> 2, sb & 1
    sign = 1 - 2 * core
    z_steps = [((z + sign * d) & 3) << 5 for d in range(4)]
    y_steps = [(((y + sign * d) & 2) << 3) | (((y + sign * d) & 1) << 1) for d in range(4)]
    x_steps = [((x + sign * d) & 3) << 2 for d in range(4)]
    cores = [core, 1 - core]

    def peer(offset):
        return z_steps[(offset >> 5) & 3] | y_steps[(offset >> 3) & 3] | x_steps[(offset >> 1) & 3] | cores[offset & 1]

    loads = [
        pltpu.make_async_copy(ref, ins.at[i], in_sem.at[i]) for i, ref in enumerate((q_hbm, k_hbm, v_hbm, c_hbm, f_hbm))
    ]
    loads.append(pltpu.make_async_copy(skip_hbm, skip, in_sem.at[5]))
    for load in loads:
        load.start()
    barrier = pltpu.get_barrier_semaphore()
    for offset in ORDER:
        pl.semaphore_signal(barrier, 1, device_id=peer(offset), device_id_type=LOGICAL)
    pairs = (
        (spread_hbm, spread_table), (gather_hbm, gather_table), (inners_hbm, inners), (turns_hbm, turns),
        (twists_hbm, twists),
    )
    constants = [pltpu.make_async_copy(a, b, const_sem.at[i]) for i, (a, b) in enumerate(pairs)]
    for load in constants:
        load.start()
    for load in loads:
        load.wait()
    gated, upstream = ins[1] * ins[2], ins[3] * ins[0]
    for number, signal in enumerate((gated, ins[4], upstream)):
        for half in range(2):
            outgoing[:, 2 * number + half, :] = signal[half * HALF : (half + 1) * HALF, :].T
    ins[0] = skip[...][None, :] * upstream
    ins[4] = skip[...][None, :] * gated

    for load in constants:
        load.wait()
    for table, target in ((spread_table, spread), (gather_table, gather)):
        high, low = split(table[...])
        width = table.shape[1]
        target[:, :width] = high
        target[:, width : 2 * width] = high
        target[:, 2 * width :] = low
    real_high, real_low = split(inners[:, :HALF])
    imag_high, imag_low = split(inners[:, HALF:])
    for base, real, imag in ((0, real_high, imag_high), (BLOCK, real_high, imag_high), (2 * BLOCK, real_low, imag_low)):
        for table, right, left in ((forward, imag, -imag), (inverse, -imag, imag)):
            table[base : base + HALF, :HALF] = real
            table[base : base + HALF, HALF:] = right
            table[base + HALF : base + BLOCK, :HALF] = left
            table[base + HALF : base + BLOCK, HALF:] = real

    def send(source, target, phase, other):
        pltpu.make_async_remote_copy(
            src_ref=source.at[other],
            dst_ref=target.at[me],
            send_sem=send_sem.at[phase],
            recv_sem=recv_sem.at[phase],
            device_id=other,
            device_id_type=LOGICAL,
        ).start()

    def receive(source, target, phase):
        own = pltpu.make_async_copy(source.at[me], target.at[me], own_sem.at[phase])
        own.start()
        own.wait()
        landed = target.at[pl.ds(0, DEVICES - 1)]
        pltpu.make_async_copy(landed, landed, recv_sem.at[phase]).wait()

    pl.semaphore_wait(barrier, DEVICES - 1)
    for offset in ORDER:
        send(outgoing, arrived, 0, peer(offset))
    receive(outgoing, arrived, 0)

    turn_real, turn_imag = turns[:HALF, :], turns[HALF:, :]
    twist_real, twist_imag = twists[0:1, :], twists[1:2, :]
    high, low = split(jnp.concatenate([arrived[:, row, :] for row in range(ROWS)], 1))
    first = dot(spread[...], jnp.concatenate([high, low, high], 0))
    parts = []
    for number in range(3):
        columns = slice(number * BLOCK, (number + 1) * BLOCK)
        real, imag = first[:HALF, columns], first[HALF:, columns]
        real, imag = real * turn_real - imag * turn_imag, real * turn_imag + imag * turn_real
        parts.append(jnp.concatenate([real[:, :HALF] + real[:, HALF:], imag[:, :HALF] + imag[:, HALF:]], 1))
        real, imag = real[:, :HALF] - real[:, HALF:], imag[:, :HALF] - imag[:, HALF:]
        parts.append(jnp.concatenate([real * twist_real - imag * twist_imag, real * twist_imag + imag * twist_real], 1))
    high, low = split(jnp.concatenate(parts, 0))
    spectra = dot(jnp.concatenate([high, low, high], 1), forward[...])
    gated_part, filter_part, upstream_part = (spectra[i * BLOCK : (i + 1) * BLOCK, :] for i in range(3))
    products = (
        product(filter_part, gated_part, False),
        product(filter_part, upstream_part, True),
        product(gated_part, upstream_part, True),
    )
    high, low = split(jnp.concatenate(products, 0))
    first = dot(jnp.concatenate([high, low, high], 1), inverse[...])
    parts = []
    for number in range(3):
        even = first[number * BLOCK : number * BLOCK + HALF, :]
        odd = first[number * BLOCK + HALF : (number + 1) * BLOCK, :]
        real, imag = odd[:, :HALF], odd[:, HALF:]
        real, imag = real * twist_real + imag * twist_imag, imag * twist_real - real * twist_imag
        real = jnp.concatenate([even[:, :HALF] + real, even[:, :HALF] - real], 1)
        imag = jnp.concatenate([even[:, HALF:] + imag, even[:, HALF:] - imag], 1)
        parts.append(jnp.concatenate([real * turn_real + imag * turn_imag, imag * turn_real - real * turn_imag], 0))
    high, low = split(jnp.concatenate(parts, 1))
    convolved = dot(gather[...], jnp.concatenate([high, low, high], 0))
    for row in range(ROWS):
        results[:, row, :] = convolved[:, row * HALF : (row + 1) * HALF]

    for to_z, step_y, to_x, step_core in returns():
        other = (to_z << 5) | y_steps[step_y] | (to_x << 2) | cores[step_core]
        if step_y == 0 and step_core == 0:
            pl.when(other != me)(lambda other=other: send(results, returned, 1, other))
        else:
            send(results, returned, 1, other)
    receive(results, returned, 1)
    for phase, source in enumerate((outgoing, results)):
        sent = source.at[pl.ds(0, DEVICES - 1)]
        pltpu.make_async_copy(sent, sent, send_sem.at[phase]).wait()


def finish_kernel(returned, ins, gq_hbm, gk_hbm, gv_hbm, gf_hbm, outs, sems):
    copies = []
    for half in range(2):
        rows = pl.ds(half * HALF, HALF)
        response = returned[:, half, :].T + ins[4, rows, :]
        back_signal = returned[:, 2 + half, :].T + ins[0, rows, :]
        outs[0, rows, :] = ins[3, rows, :] * response
        outs[1, rows, :] = back_signal * ins[2, rows, :]
        outs[2, rows, :] = back_signal * ins[1, rows, :]
        outs[3, rows, :] = returned[:, 4 + half, :].T
        for i, out in enumerate((gq_hbm, gk_hbm, gv_hbm, gf_hbm)):
            copies.append(pltpu.make_async_copy(outs.at[i, rows], out.at[rows], sems.at[i, half]))
            copies[-1].start()
    for copy in copies:
        copy.wait()


def local(queries, keys, values, cotangent, filt, skip):
    constants = tables()
    buffer = (DEVICES, ROWS, HALF)
    block = jax.ShapeDtypeStruct((BLOCK, DEVICES), jnp.float32)
    operands = (queries, keys, values, cotangent, filt, skip, *map(jnp.asarray, constants))
    returned, kept = pl.pallas_call(
        exchange_kernel,
        out_shape=(
            jax.ShapeDtypeStruct(buffer, jnp.float32),
            jax.ShapeDtypeStruct((5, BLOCK, DEVICES), jnp.float32),
        ),
        in_specs=[pl.BlockSpec(memory_space=pltpu.HBM)] * len(operands),
        out_specs=[pl.BlockSpec(memory_space=pltpu.VMEM)] * 2,
        scratch_shapes=[
            pltpu.VMEM((DEVICES,), jnp.float32),
            *[pltpu.VMEM(c.shape, jnp.float32) for c in constants],
            pltpu.VMEM((BLOCK, 3 * DEVICES), bfloat16),
            pltpu.VMEM((DEVICES, 3 * BLOCK), bfloat16),
            pltpu.VMEM((3 * BLOCK, BLOCK), bfloat16),
            pltpu.VMEM((3 * BLOCK, BLOCK), bfloat16),
            *[pltpu.VMEM(buffer, jnp.float32)] * 3,
            pltpu.SemaphoreType.DMA((6,)),
            pltpu.SemaphoreType.DMA((len(constants),)),
            pltpu.SemaphoreType.DMA((2,)),
            pltpu.SemaphoreType.DMA((2,)),
            pltpu.SemaphoreType.DMA((2,)),
        ],
        compiler_params=pltpu.CompilerParams(
            collective_id=0, has_side_effects=True, vmem_limit_bytes=40 * 1024 * 1024
        ),
        name="channel_convolutions",
    )(*[pltpu.with_memory_space_constraint(operand, pltpu.HBM) for operand in operands])
    return pl.pallas_call(
        finish_kernel,
        out_shape=(block,) * 4,
        in_specs=[pl.BlockSpec(memory_space=pltpu.VMEM)] * 2,
        out_specs=[pl.BlockSpec(memory_space=pltpu.HBM)] * 4,
        scratch_shapes=[pltpu.VMEM((4, BLOCK, DEVICES), jnp.float32), pltpu.SemaphoreType.DMA((4, 2))],
        compiler_params=pltpu.CompilerParams(vmem_limit_bytes=8 * 1024 * 1024),
        name="gates",
    )(returned, kept)


def solution(mesh):
    in_specs = (P(("sa", "sb"), None),) * 5 + (P(),)
    out_specs = (P(("sa", "sb"), None),) * 4
    return jax.shard_map(local, mesh=mesh, in_specs=in_specs, out_specs=out_specs, check_vma=False)
```

time: 31 us -> 28.6 us (0.923)
  Pallas kernels: 30.2 us -> 27.8 us
    pallas_call x1, Pallas kernels: 29.1 us -> 26.7 us  [local(): pl.pallas_call(exchange_kernel, out_shape=(jax.ShapeDtypeStruct(buffer, j...]
where the time goes in v2:
time: 28.6 us; the launch traced here: 28.4 us
  Pallas kernels  27.8 us (97%)
  between operations  0.64 us (2%)
    pallas_call x1, Pallas kernels, local(): pl.pallas_call(exchange_kernel, out_shape=(jax.ShapeDtypeStruct(buffer, j...  26.7 us
    pallas_call x1, Pallas kernels, local(): pl.pallas_call(finish_kernel, out_shape=(block,) * 4, in_specs=[pl.BlockS...  1.06 us

profile of v2, /device:TPU:1, one launch (start us, length us, event | category | flops | bytes accessed | tf_op | source)
XLA Modules:
  0.0 28.4 jit_solution(1979827356382999325)
XLA Ops:
  0.6 26.7 %channel_convolutions.1 = (f32[128,6,128]{2,1,0:T(8,128)S(1)}, f32[5,256,128]{2,1,0:T(8,128)S(1)}) custom-call(f32[256,128]{1,0:T(8,128)} %q_hbm.1, f32[256,128]{1,0:T(8,128)} %k_hbm.1, f32[256,128]{1,0:T(8,128)} %v_hbm.1, f32[256,128]{1,0:T(8,128)} %c_hbm.1, f32[256,128]{1,0:T(8,128)} %f_hbm.1, f32[128]{0:T(128)} %skip_hbm.1, ...), custom_call_target="tpu_custom_call" | custom-call | tf_op jit(solution)/shard_map/channel_convolutions/pallas_call | solution.py:222
  27.4 1.1 %gates.1 = (f32[256,128]{1,0:T(8,128)}, f32[256,128]{1,0:T(8,128)}, f32[256,128]{1,0:T(8,128)}, f32[256,128]{1,0:T(8,128)}) custom-call(f32[128,6,128]{2,1,0:T(8,128)S(1)} %get-tuple-element.6.returned, f32[5,256,128]{2,1,0:T(8,128)S(1)} %get-tuple-element.7.ins), custom_call_target="tpu_custom_call" | custom-call | tf_op jit(solution)/shard_map/gates/pallas_call | solution.py:249

commit v3 on v2

--- a/solution.py
+++ b/solution.py
@@ -107,6 +107,26 @@
     for number, signal in enumerate((gated, ins[4], upstream)):
         for half in range(2):
             outgoing[:, 2 * number + half, :] = signal[half * HALF : (half + 1) * HALF, :].T
+    def send(source, target, phase, other):
+        pltpu.make_async_remote_copy(
+            src_ref=source.at[other],
+            dst_ref=target.at[me],
+            send_sem=send_sem.at[phase],
+            recv_sem=recv_sem.at[phase],
+            device_id=other,
+            device_id_type=LOGICAL,
+        ).start()
+
+    def receive(source, target, phase):
+        own = pltpu.make_async_copy(source.at[me], target.at[me], own_sem.at[phase])
+        own.start()
+        own.wait()
+        landed = target.at[pl.ds(0, DEVICES - 1)]
+        pltpu.make_async_copy(landed, landed, recv_sem.at[phase]).wait()
+
+    pl.semaphore_wait(barrier, DEVICES - 1)
+    for offset in ORDER:
+        send(outgoing, arrived, 0, peer(offset))
     ins[0] = skip[...][None, :] * upstream
     ins[4] = skip[...][None, :] * gated
 
@@ -127,63 +147,52 @@
             table[base + HALF : base + BLOCK, :HALF] = left
             table[base + HALF : base + BLOCK, HALF:] = real
 
-    def send(source, target, phase, other):
-        pltpu.make_async_remote_copy(
-            src_ref=source.at[other],
-            dst_ref=target.at[me],
-            send_sem=send_sem.at[phase],
-            recv_sem=recv_sem.at[phase],
-            device_id=other,
-            device_id_type=LOGICAL,
-        ).start()
-
-    def receive(source, target, phase):
-        own = pltpu.make_async_copy(source.at[me], target.at[me], own_sem.at[phase])
-        own.start()
-        own.wait()
-        landed = target.at[pl.ds(0, DEVICES - 1)]
-        pltpu.make_async_copy(landed, landed, recv_sem.at[phase]).wait()
-
-    pl.semaphore_wait(barrier, DEVICES - 1)
-    for offset in ORDER:
-        send(outgoing, arrived, 0, peer(offset))
     receive(outgoing, arrived, 0)
 
     turn_real, turn_imag = turns[:HALF, :], turns[HALF:, :]
     twist_real, twist_imag = twists[0:1, :], twists[1:2, :]
-    high, low = split(jnp.concatenate([arrived[:, row, :] for row in range(ROWS)], 1))
-    first = dot(spread[...], jnp.concatenate([high, low, high], 0))
-    parts = []
-    for number in range(3):
-        columns = slice(number * BLOCK, (number + 1) * BLOCK)
-        real, imag = first[:HALF, columns], first[HALF:, columns]
+
+    def along_blocks(matrix, x):
+        high, low = split(x)
+        return dot(matrix[...], jnp.concatenate([high, low, high], 0))
+
+    def along_positions(x, matrix):
+        high, low = split(x)
+        return dot(jnp.concatenate([high, low, high], 1), matrix[...])
+
+    def turned(first):
+        real, imag = first[:HALF, :], first[HALF:, :]
         real, imag = real * turn_real - imag * turn_imag, real * turn_imag + imag * turn_real
-        parts.append(jnp.concatenate([real[:, :HALF] + real[:, HALF:], imag[:, :HALF] + imag[:, HALF:]], 1))
+        even = jnp.concatenate([real[:, :HALF] + real[:, HALF:], imag[:, :HALF] + imag[:, HALF:]], 1)
         real, imag = real[:, :HALF] - real[:, HALF:], imag[:, :HALF] - imag[:, HALF:]
-        parts.append(jnp.concatenate([real * twist_real - imag * twist_imag, real * twist_imag + imag * twist_real], 1))
-    high, low = split(jnp.concatenate(parts, 0))
-    spectra = dot(jnp.concatenate([high, low, high], 1), forward[...])
-    gated_part, filter_part, upstream_part = (spectra[i * BLOCK : (i + 1) * BLOCK, :] for i in range(3))
-    products = (
-        product(filter_part, gated_part, False),
-        product(filter_part, upstream_part, True),
-        product(gated_part, upstream_part, True),
-    )
-    high, low = split(jnp.concatenate(products, 0))
-    first = dot(jnp.concatenate([high, low, high], 1), inverse[...])
-    parts = []
-    for number in range(3):
-        even = first[number * BLOCK : number * BLOCK + HALF, :]
-        odd = first[number * BLOCK + HALF : (number + 1) * BLOCK, :]
+        return even, jnp.concatenate([real * twist_real - imag * twist_imag, real * twist_imag + imag * twist_real], 1)
+
+    def turned_back(even, odd):
         real, imag = odd[:, :HALF], odd[:, HALF:]
         real, imag = real * twist_real + imag * twist_imag, imag * twist_real - real * twist_imag
         real = jnp.concatenate([even[:, :HALF] + real, even[:, :HALF] - real], 1)
         imag = jnp.concatenate([even[:, HALF:] + imag, even[:, HALF:] - imag], 1)
-        parts.append(jnp.concatenate([real * turn_real + imag * turn_imag, imag * turn_real - real * turn_imag], 0))
-    high, low = split(jnp.concatenate(parts, 1))
-    convolved = dot(gather[...], jnp.concatenate([high, low, high], 0))
-    for row in range(ROWS):
-        results[:, row, :] = convolved[:, row * HALF : (row + 1) * HALF]
+        return jnp.concatenate([real * turn_real + imag * turn_imag, imag * turn_real - real * turn_imag], 0)
+
+    firsts = [
+        along_blocks(spread, jnp.concatenate([arrived[:, row, :], arrived[:, row + 1, :]], 1)) for row in (0, 2, 4)
+    ]
+    parts = [turned(first) for first in firsts]
+    gated_part, filter_part, upstream_part = ([along_positions(half, forward) for half in part] for part in parts)
+    products = [
+        [product(a, b, conjugate) for a, b in zip(left, right)]
+        for left, right, conjugate in (
+            (filter_part, gated_part, False),
+            (filter_part, upstream_part, True),
+            (gated_part, upstream_part, True),
+        )
+    ]
+    firsts = [[along_positions(half, inverse) for half in part] for part in products]
+    parts = [turned_back(even, odd) for even, odd in firsts]
+    for number, part in enumerate(parts):
+        convolved = along_blocks(gather, part)
+        for half in range(2):
+            results[:, 2 * number + half, :] = convolved[:, half * HALF : (half + 1) * HALF]
 
     for to_z, step_y, to_x, step_core in returns():
         other = (to_z << 5) | y_steps[step_y] | (to_x << 2) | cores[step_core]

time: 28.6 us -> 28.1 us (0.983)
  Pallas kernels: 27.8 us -> 27.3 us
    pallas_call x1, Pallas kernels: 26.7 us -> 26.3 us  [local(): pl.pallas_call(exchange_kernel, out_shape=(jax.ShapeDtypeStruct(buffer, j...]
where the time goes in v3:
time: 28.1 us; the launch traced here: 28 us
  Pallas kernels  27.3 us (97%)
  between operations  0.64 us (2%)
    pallas_call x1, Pallas kernels, local(): pl.pallas_call(exchange_kernel, out_shape=(jax.ShapeDtypeStruct(buffer, j...  26.3 us
    pallas_call x1, Pallas kernels, local(): pl.pallas_call(finish_kernel, out_shape=(block,) * 4, in_specs=[pl.BlockS...  1.06 us

profile of v3, /device:TPU:1, one launch (start us, length us, event | category | flops | bytes accessed | tf_op | source)
XLA Modules:
  0.0 28.0 jit_solution(10624586491815839351)
XLA Ops:
  0.6 26.3 %channel_convolutions.1 = (f32[128,6,128]{2,1,0:T(8,128)S(1)}, f32[5,256,128]{2,1,0:T(8,128)S(1)}) custom-call(f32[256,128]{1,0:T(8,128)} %q_hbm.1, f32[256,128]{1,0:T(8,128)} %k_hbm.1, f32[256,128]{1,0:T(8,128)} %v_hbm.1, f32[256,128]{1,0:T(8,128)} %c_hbm.1, f32[256,128]{1,0:T(8,128)} %f_hbm.1, f32[128]{0:T(128)} %skip_hbm.1, ...), custom_call_target="tpu_custom_call" | custom-call | tf_op jit(solution)/shard_map/channel_convolutions/pallas_call | solution.py:231
  26.9 1.1 %gates.1 = (f32[256,128]{1,0:T(8,128)}, f32[256,128]{1,0:T(8,128)}, f32[256,128]{1,0:T(8,128)}, f32[256,128]{1,0:T(8,128)}) custom-call(f32[128,6,128]{2,1,0:T(8,128)S(1)} %get-tuple-element.6.returned, f32[5,256,128]{2,1,0:T(8,128)S(1)} %get-tuple-element.7.ins), custom_call_target="tpu_custom_call" | custom-call | tf_op jit(solution)/shard_map/gates/pallas_call | solution.py:258

commit v4 on v3

--- a/solution.py
+++ b/solution.py
@@ -45,7 +45,10 @@
     return sorted(places, key=lambda p: (BEHIND[0][p[0]] + BEHIND[1][p[2]] - 0.64 * RING[p[1]], -p[3]))
 
 
-ORDER = sorted(range(1, DEVICES), key=lambda offset: (-hops(offset), (offset * 77) % DEVICES))
+ORDER = sorted(
+    range(1, DEVICES),
+    key=lambda s: (-(s >> 6), -RING[(s >> 3) & 3] - RING[(s >> 1) & 3] - 0.5 * ((s >> 5) & 1), (s * 77) % DEVICES),
+)
 
 
 def split(x):
@@ -77,7 +80,7 @@
     z, y = sa >> 1, ((sa & 1) << 1) | ((sb >> 1) & 1)
     x, core = sb >> 2, sb & 1
     sign = 1 - 2 * core
-    z_steps = [((z + sign * d) & 3) << 5 for d in range(4)]
+    z_steps = [(z ^ d) << 5 for d in range(4)]
     y_steps = [(((y + sign * d) & 2) << 3) | (((y + sign * d) & 1) << 1) for d in range(4)]
     x_steps = [((x + sign * d) & 3) << 2 for d in range(4)]
     cores = [core, 1 - core]

time: 28.1 us -> 27.9 us (level)
  no operation moved by 1% of the time
where the time goes in v4:
time: 27.9 us; the launch traced here: 27.8 us
  Pallas kernels  27.1 us (97%)
  between operations  0.64 us (2%)
    pallas_call x1, Pallas kernels, local(): pl.pallas_call(exchange_kernel, out_shape=(jax.ShapeDtypeStruct(buffer, j...  26.1 us
    pallas_call x1, Pallas kernels, local(): pl.pallas_call(finish_kernel, out_shape=(block,) * 4, in_specs=[pl.BlockS...  1.06 us

profile of v4, /device:TPU:1, one launch (start us, length us, event | category | flops | bytes accessed | tf_op | source)
XLA Modules:
  0.0 27.8 jit_solution(16399995381052384658)
XLA Ops:
  0.6 26.1 %channel_convolutions.1 = (f32[128,6,128]{2,1,0:T(8,128)S(1)}, f32[5,256,128]{2,1,0:T(8,128)S(1)}) custom-call(f32[256,128]{1,0:T(8,128)} %q_hbm.1, f32[256,128]{1,0:T(8,128)} %k_hbm.1, f32[256,128]{1,0:T(8,128)} %v_hbm.1, f32[256,128]{1,0:T(8,128)} %c_hbm.1, f32[256,128]{1,0:T(8,128)} %f_hbm.1, f32[128]{0:T(128)} %skip_hbm.1, ...), custom_call_target="tpu_custom_call" | custom-call | tf_op jit(solution)/shard_map/channel_convolutions/pallas_call | solution.py:234
  26.7 1.1 %gates.1 = (f32[256,128]{1,0:T(8,128)}, f32[256,128]{1,0:T(8,128)}, f32[256,128]{1,0:T(8,128)}, f32[256,128]{1,0:T(8,128)}) custom-call(f32[128,6,128]{2,1,0:T(8,128)S(1)} %get-tuple-element.6.returned, f32[5,256,128]{2,1,0:T(8,128)S(1)} %get-tuple-element.7.ins), custom_call_target="tpu_custom_call" | custom-call | tf_op jit(solution)/shard_map/gates/pallas_call | solution.py:261

commit v5 on v4

--- a/solution.py
+++ b/solution.py
@@ -203,10 +203,10 @@
             pl.when(other != me)(lambda other=other: send(results, returned, 1, other))
         else:
             send(results, returned, 1, other)
-    receive(results, returned, 1)
     for phase, source in enumerate((outgoing, results)):
         sent = source.at[pl.ds(0, DEVICES - 1)]
         pltpu.make_async_copy(sent, sent, send_sem.at[phase]).wait()
+    receive(results, returned, 1)
 
 
 def finish_kernel(returned, ins, gq_hbm, gk_hbm, gv_hbm, gf_hbm, outs, sems):

time: 27.9 us -> 27.9 us (level)
  no operation moved by 1% of the time
where the time goes in v5:
time: 27.9 us; the launch traced here: 27.8 us
  Pallas kernels  27.1 us (97%)
  between operations  0.64 us (2%)
    pallas_call x1, Pallas kernels, local(): pl.pallas_call(exchange_kernel, out_shape=(jax.ShapeDtypeStruct(buffer, j...  26.1 us
    pallas_call x1, Pallas kernels, local(): pl.pallas_call(finish_kernel, out_shape=(block,) * 4, in_specs=[pl.BlockS...  1.06 us

profile of v5, /device:TPU:1, one launch (start us, length us, event | category | flops | bytes accessed | tf_op | source)
XLA Modules:
  0.0 27.8 jit_solution(12486234643459887847)
XLA Ops:
  0.6 26.1 %channel_convolutions.1 = (f32[128,6,128]{2,1,0:T(8,128)S(1)}, f32[5,256,128]{2,1,0:T(8,128)S(1)}) custom-call(f32[256,128]{1,0:T(8,128)} %q_hbm.1, f32[256,128]{1,0:T(8,128)} %k_hbm.1, f32[256,128]{1,0:T(8,128)} %v_hbm.1, f32[256,128]{1,0:T(8,128)} %c_hbm.1, f32[256,128]{1,0:T(8,128)} %f_hbm.1, f32[128]{0:T(128)} %skip_hbm.1, ...), custom_call_target="tpu_custom_call" | custom-call | tf_op jit(solution)/shard_map/channel_convolutions/pallas_call | solution.py:234
  26.7 1.1 %gates.1 = (f32[256,128]{1,0:T(8,128)}, f32[256,128]{1,0:T(8,128)}, f32[256,128]{1,0:T(8,128)}, f32[256,128]{1,0:T(8,128)}) custom-call(f32[128,6,128]{2,1,0:T(8,128)S(1)} %get-tuple-element.6.returned, f32[5,256,128]{2,1,0:T(8,128)S(1)} %get-tuple-element.7.ins), custom_call_target="tpu_custom_call" | custom-call | tf_op jit(solution)/shard_map/gates/pallas_call | solution.py:261

commit v6 on v5

--- a/solution.py
+++ b/solution.py
@@ -88,15 +88,15 @@
     def peer(offset):
         return z_steps[(offset >> 5) & 3] | y_steps[(offset >> 3) & 3] | x_steps[(offset >> 1) & 3] | cores[offset & 1]
 
+    barrier = pltpu.get_barrier_semaphore()
+    for offset in ORDER:
+        pl.semaphore_signal(barrier, 1, device_id=peer(offset), device_id_type=LOGICAL)
     loads = [
         pltpu.make_async_copy(ref, ins.at[i], in_sem.at[i]) for i, ref in enumerate((q_hbm, k_hbm, v_hbm, c_hbm, f_hbm))
     ]
     loads.append(pltpu.make_async_copy(skip_hbm, skip, in_sem.at[5]))
     for load in loads:
         load.start()
-    barrier = pltpu.get_barrier_semaphore()
-    for offset in ORDER:
-        pl.semaphore_signal(barrier, 1, device_id=peer(offset), device_id_type=LOGICAL)
     pairs = (
         (spread_hbm, spread_table), (gather_hbm, gather_table), (inners_hbm, inners), (turns_hbm, turns),
         (twists_hbm, twists),

time: 27.9 us -> 27.9 us (level)
  no operation moved by 1% of the time
where the time goes in v6:
time: 27.9 us; the launch traced here: 27.8 us
  Pallas kernels  27.1 us (97%)
  between operations  0.64 us (2%)
    pallas_call x1, Pallas kernels, local(): pl.pallas_call(exchange_kernel, out_shape=(jax.ShapeDtypeStruct(buffer, j...  26.1 us
    pallas_call x1, Pallas kernels, local(): pl.pallas_call(finish_kernel, out_shape=(block,) * 4, in_specs=[pl.BlockS...  1.06 us

profile of v6, /device:TPU:1, one launch (start us, length us, event | category | flops | bytes accessed | tf_op | source)
XLA Modules:
  0.0 27.8 jit_solution(890854857579011269)
XLA Ops:
  0.6 26.1 %channel_convolutions.1 = (f32[128,6,128]{2,1,0:T(8,128)S(1)}, f32[5,256,128]{2,1,0:T(8,128)S(1)}) custom-call(f32[256,128]{1,0:T(8,128)} %q_hbm.1, f32[256,128]{1,0:T(8,128)} %k_hbm.1, f32[256,128]{1,0:T(8,128)} %v_hbm.1, f32[256,128]{1,0:T(8,128)} %c_hbm.1, f32[256,128]{1,0:T(8,128)} %f_hbm.1, f32[128]{0:T(128)} %skip_hbm.1, ...), custom_call_target="tpu_custom_call" | custom-call | tf_op jit(solution)/shard_map/channel_convolutions/pallas_call | solution.py:234
  26.7 1.1 %gates.1 = (f32[256,128]{1,0:T(8,128)}, f32[256,128]{1,0:T(8,128)}, f32[256,128]{1,0:T(8,128)}, f32[256,128]{1,0:T(8,128)}) custom-call(f32[128,6,128]{2,1,0:T(8,128)S(1)} %get-tuple-element.6.returned, f32[5,256,128]{2,1,0:T(8,128)S(1)} %get-tuple-element.7.ins), custom_call_target="tpu_custom_call" | custom-call | tf_op jit(solution)/shard_map/gates/pallas_call | solution.py:261

commit v7 on v5

--- a/solution.py
+++ b/solution.py
@@ -197,6 +197,8 @@
         for half in range(2):
             results[:, 2 * number + half, :] = convolved[:, half * HALF : (half + 1) * HALF]
 
+    own = pltpu.make_async_copy(results.at[me], returned.at[me], own_sem.at[1])
+    own.start()
     for to_z, step_y, to_x, step_core in returns():
         other = (to_z << 5) | y_steps[step_y] | (to_x << 2) | cores[step_core]
         if step_y == 0 and step_core == 0:
@@ -206,7 +208,9 @@
     for phase, source in enumerate((outgoing, results)):
         sent = source.at[pl.ds(0, DEVICES - 1)]
         pltpu.make_async_copy(sent, sent, send_sem.at[phase]).wait()
-    receive(results, returned, 1)
+    own.wait()
+    landed = returned.at[pl.ds(0, DEVICES - 1)]
+    pltpu.make_async_copy(landed, landed, recv_sem.at[1]).wait()
 
 
 def finish_kernel(returned, ins, gq_hbm, gk_hbm, gv_hbm, gf_hbm, outs, sems):

time: 27.9 us -> 27.9 us (level)
  no operation moved by 1% of the time
where the time goes in v7:
time: 27.9 us; the launch traced here: 27.8 us
  Pallas kernels  27.1 us (97%)
  between operations  0.64 us (2%)
    pallas_call x1, Pallas kernels, local(): pl.pallas_call(exchange_kernel, out_shape=(jax.ShapeDtypeStruct(buffer, j...  26.1 us
    pallas_call x1, Pallas kernels, local(): pl.pallas_call(finish_kernel, out_shape=(block,) * 4, in_specs=[pl.BlockS...  1.06 us

profile of v7, /device:TPU:1, one launch (start us, length us, event | category | flops | bytes accessed | tf_op | source)
XLA Modules:
  0.0 27.8 jit_solution(15933728491999423448)
XLA Ops:
  0.6 26.1 %channel_convolutions.1 = (f32[128,6,128]{2,1,0:T(8,128)S(1)}, f32[5,256,128]{2,1,0:T(8,128)S(1)}) custom-call(f32[256,128]{1,0:T(8,128)} %q_hbm.1, f32[256,128]{1,0:T(8,128)} %k_hbm.1, f32[256,128]{1,0:T(8,128)} %v_hbm.1, f32[256,128]{1,0:T(8,128)} %c_hbm.1, f32[256,128]{1,0:T(8,128)} %f_hbm.1, f32[128]{0:T(128)} %skip_hbm.1, ...), custom_call_target="tpu_custom_call" | custom-call | tf_op jit(solution)/shard_map/channel_convolutions/pallas_call | solution.py:238
  26.7 1.1 %gates.1 = (f32[256,128]{1,0:T(8,128)}, f32[256,128]{1,0:T(8,128)}, f32[256,128]{1,0:T(8,128)}, f32[256,128]{1,0:T(8,128)}) custom-call(f32[128,6,128]{2,1,0:T(8,128)S(1)} %get-tuple-element.6.returned, f32[5,256,128]{2,1,0:T(8,128)S(1)} %get-tuple-element.7.ins), custom_call_target="tpu_custom_call" | custom-call | tf_op jit(solution)/shard_map/gates/pallas_call | solution.py:265
